TPU v7x, 128 devices: a whole 4x4x4 slice. The times are simulated.
128 devices in a mesh: expert: 64 (over z, y, x), replica: 2 (over core).
Axes of the slice: x: 4, y: 4, z: 4, core: 2. Of those that a mesh axis runs over, the one named last changes fastest.
Arguments:
- samples: float32 [131072, 256], P(('expert', 'replica')), may hold values from -6 to 6
- routes: int32 [131072, 1], P(('expert', 'replica')), may hold values from 0 to 63; in each aligned block of 1024 rows (0 to 1023, 1024 to 2047, ...) at most 32 rows name the same one
- cotangent: float32 [131072, 256], P(('expert', 'replica')), may hold values from -6 to 6
- weights: float32 [7, 64, 256, 256], P(None, 'expert', 'replica'), may hold values from -0.375 to 0.375
- moment_one: float32 [7, 64, 256, 256], P(None, 'expert', 'replica'), may hold values from -6 to 6
- moment_two: float32 [7, 64, 256, 256], P(None, 'expert', 'replica'), may hold values from 1 to 30
Outputs:
- outputs: float32 [131072, 256], P(('expert', 'replica'))
- new_weights: float32 [7, 64, 256, 256], P(None, 'expert', 'replica')
- new_moment_one: float32 [7, 64, 256, 256], P(None, 'expert', 'replica')
- new_moment_two: float32 [7, 64, 256, 256], P(None, 'expert', 'replica')
Inputs may be any that keep to these rules, and one draw needn't show every extreme that they name: `routes`: among the 1024 rows of one device no expert is chosen by more than 32 rows; some expert is chosen by exactly 32 rows of some device.
All inputs are finite; a program needn't handle non-finite values.
Results may differ from a plain program's by a relative error of at most 0.0002.
Values sent between devices are 32-bit elements; how exact they have to be, the bound alone decides.
A program may use at most 128 MiB of HBM per device.

v0:
```python
import jax
import jax.numpy as jnp
from jax import lax
from jax.experimental import pallas as pl
from jax.experimental.pallas import tpu as pltpu
from jax.sharding import PartitionSpec as P

MESH = pl.DeviceIdType.MESH
CORR_ONE = 0.9999734386011124
CORR_TWO = 0.09520785288629038
F32 = jnp.float32
BF16 = jnp.bfloat16

SIDE = 4
PEERS = SIDE**3
CAP = 32
WIDTH = 256
ROWS = 1024
LAYERS = 7
HALF = WIDTH // 2
PER = 8
GROUPS = PEERS // PER
TILE = PER * CAP
STRIDE = 37


def split(value):
    high = value.astype(BF16)
    low = (value - high.astype(F32)).astype(BF16)
    return high, low


def mm(a, b):
    return lax.dot_general(a, b, (((1,), (0,)), ((), ())), preferred_element_type=F32)


def mm_nt(a, b):
    return lax.dot_general(a, b, (((1,), (1,)), ((), ())), preferred_element_type=F32)


def mm_tn(a, b):
    return lax.dot_general(a, b, (((0,), (0,)), ((), ())), preferred_element_type=F32)


def peer(me, k):
    off = (k * STRIDE) % PEERS
    x = (me + off) % SIDE
    y = (me // SIDE + off // SIDE) % SIDE
    z = (me // (SIDE * SIDE) + off // (SIDE * SIDE)) % SIDE
    return z * (SIDE * SIDE) + y * SIDE + x


def peer_back(me, k):
    off = (k * STRIDE) % PEERS
    x = (me + SIDE - off % SIDE) % SIDE
    y = (me // SIDE + SIDE - (off // SIDE) % SIDE) % SIDE
    z = (me // (SIDE * SIDE) + SIDE - off // (SIDE * SIDE)) % SIDE
    return z * (SIDE * SIDE) + y * SIDE + x


def wanted(me, group, shape, axis):
    j = lax.broadcasted_iota(jnp.int32, shape, axis) + group * TILE
    k = lax.shift_right_logical(j, 5)
    off = (k * STRIDE) & (PEERS - 1)
    x = (me + off) & 3
    y = (lax.shift_right_logical(off, 2) + me // SIDE) & 3
    z = (lax.shift_right_logical(off, 4) + me // (SIDE * SIDE)) & 3
    return (z * 16 + y * 4 + x) * CAP + (j & (CAP - 1))


def kernel(
    routes, samples, cotangent, weights, one, two,
    outputs, new_w, new_one, new_two,
    sv, cv, wf, m1, m2, wh, wl, sp, cp, arr, arc, ret, ah, al, slope, grads, got, slot, slot_t, o_w, o_1, o_2,
    in_sem, out_sem, send_sem, recv_sem, w_sem, g_sem,
):
    me = lax.axis_index("expert")
    rep = lax.axis_index("replica")
    other = 1 - rep

    loads = [
        pltpu.make_async_copy(src, dst, in_sem.at[i])
        for i, (src, dst) in enumerate(
            ((samples, sv), (weights, wf.at[rep]), (cotangent, cv), (one, m1), (two, m2))
        )
    ]
    for load in loads:
        load.start()

    barrier = pltpu.get_barrier_semaphore()

    def greet(k, carry):
        pl.semaphore_signal(barrier, inc=1, device_id={"expert": peer_back(me, k)}, device_id_type=MESH)
        return carry

    lax.fori_loop(1, PEERS, greet, 0)
    pl.semaphore_signal(barrier, inc=1, device_id={"replica": other}, device_id_type=MESH)

    route = routes[...]
    earlier = (
        lax.broadcasted_iota(jnp.int32, (256, 256), 0) < lax.broadcasted_iota(jnp.int32, (256, 256), 1)
    ).astype(F32).astype(BF16)
    experts = lax.broadcasted_iota(jnp.int32, (PEERS, 256), 0)
    base = jnp.zeros((PEERS, 1), F32)
    for b in range(ROWS // 256):
        part = route[:, b * 256 : (b + 1) * 256]
        hot = (experts == part).astype(F32)
        before = mm(hot.astype(BF16), earlier) + base
        rank = jnp.sum(hot * before, axis=0, keepdims=True)
        base = base + jnp.sum(hot, axis=1, keepdims=True)
        slot[:, b * 256 : (b + 1) * 256] = part * CAP + rank.astype(jnp.int32)

    def remote(phase, src, dst, k, g, to):
        return pltpu.make_async_remote_copy(
            src_ref=src, dst_ref=dst, send_sem=send_sem.at[phase], recv_sem=recv_sem.at[phase, g],
            device_id={"expert": to}, device_id_type=MESH,
        )

    def send_group(phase, src, dst, g, where):
        @pl.when(g == 0)
        def _():
            pltpu.make_async_copy(src.at[0], dst.at[0], recv_sem.at[phase, 0]).start()

        @pl.when(g > 0)
        def _():
            k = g * PER
            remote(phase, src.at[k], dst.at[k], k, g, where(me, k)).start()

        def one_send(i, carry):
            k = g * PER + i
            remote(phase, src.at[k], dst.at[k], k, g, where(me, k)).start()
            return carry

        lax.fori_loop(1, PER, one_send, 0)

    def wait_group(phase, dst, g):
        block = dst.at[pl.ds(g * PER, PER)]
        remote(phase, block, block, 0, g, me).wait_recv()

    def pack_group(high, low, dst, g):
        want = wanted(me, g, (TILE, 128), 0)
        want = jnp.concatenate([want] * (ROWS // 128), axis=1)
        hot = (want == slot[...]).astype(F32).astype(BF16)
        packed = mm(hot, high) + mm(hot, low)
        dst[pl.ds(g * PER, PER)] = packed.reshape(PER, CAP, WIDTH)

    loads[0].wait()
    s_high, s_low = split(sv[...])
    loads[1].wait()
    pl.semaphore_wait(barrier, PEERS)
    weight_copy = pltpu.make_async_remote_copy(
        src_ref=wf.at[rep], dst_ref=wf.at[rep], send_sem=w_sem.at[0], recv_sem=w_sem.at[1],
        device_id={"replica": other}, device_id_type=MESH,
    )
    weight_copy.start()

    def pack_samples(g, carry):
        pack_group(s_high, s_low, sp, g)
        send_group(0, sp, arr, g, peer)
        return carry

    lax.fori_loop(0, GROUPS, pack_samples, 0)

    loads[2].wait()
    c_high, c_low = split(cv[...])

    def pack_cotangent(g, carry):
        pack_group(c_high, c_low, cp, g)
        send_group(1, cp, arc, g, peer)
        return carry

    lax.fori_loop(0, GROUPS, pack_cotangent, 0)

    slot_t[...] = jnp.transpose(jnp.broadcast_to(slot[...], (128, ROWS)))

    weight_copy.wait()

    def split_weights(layer, carry):
        for half in range(2):
            high, low = split(wf[half, layer])
            wh[layer, half * HALF : (half + 1) * HALF] = high
            wl[layer, half * HALF : (half + 1) * HALF] = low
        grads[0, layer] = jnp.zeros((HALF, WIDTH), F32)
        grads[1, layer] = jnp.zeros((HALF, WIDTH), F32)
        return carry

    lax.fori_loop(0, LAYERS, split_weights, 0)

    def forward(g, carry):
        wait_group(0, arr, g)
        rows = pl.ds(g * TILE, TILE)
        hidden = arr[pl.ds(g * PER, PER)].reshape(TILE, WIDTH)
        for layer in range(LAYERS):
            high, low = split(hidden)
            ah[layer, rows] = high
            al[layer, rows] = low
            pre = mm(high, wh[layer]) + mm(low, wh[layer]) + mm(high, wl[layer])
            if layer < LAYERS - 1:
                sigma = jax.nn.sigmoid(pre)
                hidden = pre * sigma
                slope[layer, rows] = sigma * (1.0 + pre * (1.0 - sigma))
        arr[pl.ds(g * PER, PER)] = pre.reshape(PER, CAP, WIDTH)
        send_group(2, arr, ret, g, peer_back)
        return carry

    lax.fori_loop(0, GROUPS, forward, 0)

    def backward(g, carry):
        wait_group(1, arc, g)
        rows = pl.ds(g * TILE, TILE)
        delta = arc[pl.ds(g * PER, PER)].reshape(TILE, WIDTH)
        for layer in range(LAYERS - 1, -1, -1):
            high, low = split(delta)
            a_high, a_low = ah[layer, rows], al[layer, rows]
            grad = mm_tn(a_high, high) + mm_tn(a_high, low) + mm_tn(a_low, high)
            grads[0, layer] += grad[:HALF]
            grads[1, layer] += grad[HALF:]
            if layer > 0:
                back = mm_nt(high, wh[layer]) + mm_nt(low, wh[layer]) + mm_nt(high, wl[layer])
                delta = back * slope[layer - 1, rows]
        return carry

    lax.fori_loop(0, GROUPS, backward, 0)

    grad_copy = pltpu.make_async_remote_copy(
        src_ref=grads.at[other], dst_ref=got, send_sem=g_sem.at[0], recv_sem=g_sem.at[1],
        device_id={"replica": other}, device_id_type=MESH,
    )
    grad_copy.start()
    loads[3].wait()
    loads[4].wait()
    grad_copy.wait()

    def adam(layer, carry):
        grad = grads[rep, layer] + got[layer]
        first = 0.9 * m1[layer] + 0.1 * grad
        second = 0.999 * m2[layer] + 0.001 * grad * grad
        o_1[layer] = first
        o_2[layer] = second
        o_w[layer] = wf[rep, layer] - 0.01 * (first / CORR_ONE) / (jnp.sqrt(second / CORR_TWO) + 1e-08)
        return carry

    lax.fori_loop(0, LAYERS, adam, 0)
    stores = [
        pltpu.make_async_copy(src, dst, out_sem.at[i])
        for i, (src, dst) in enumerate(((o_w, new_w), (o_1, new_one), (o_2, new_two)))
    ]
    for store in stores:
        store.start()

    outputs[...] = jnp.zeros((ROWS, WIDTH), F32)

    def unpack(g, carry):
        wait_group(2, ret, g)
        high, low = split(ret[pl.ds(g * PER, PER)].reshape(TILE, WIDTH))
        want = wanted(me, g, (8, TILE), 1)[:1]

        def some_rows(i, carry):
            rows = pl.ds(i * 256, 256)
            mine = slot_t[rows]
            mine = jnp.concatenate([mine, mine], axis=1)
            hot = (mine == want).astype(F32).astype(BF16)
            outputs[rows] += mm(hot, high) + mm(hot, low)
            return carry

        lax.fori_loop(0, ROWS // 256, some_rows, 0)
        return carry

    lax.fori_loop(0, GROUPS, unpack, 0)

    for store in stores:
        store.wait()
    for phase, src in enumerate((sp, cp, arr)):
        block = src.at[pl.ds(1, PEERS - 1)]
        remote(phase, block, block, 0, 0, me).wait_send()


def on_device(samples, routes, cotangent, weights, moment_one, moment_two):
    shard = (LAYERS, HALF, WIDTH)
    state = jax.ShapeDtypeStruct(shard, F32)
    hbm = pl.BlockSpec(memory_space=pl.ANY)
    vmem = pl.BlockSpec(memory_space=pltpu.VMEM)
    peers = (PEERS, CAP, WIDTH)
    slots = PEERS * CAP
    flops = 2 * slots * WIDTH * WIDTH * 60
    outputs, new_w, new_one, new_two = pl.pallas_call(
        kernel,
        out_shape=(jax.ShapeDtypeStruct((ROWS, WIDTH), F32), state, state, state),
        in_specs=[vmem] + [hbm] * 5,
        out_specs=(vmem, hbm, hbm, hbm),
        scratch_shapes=[
            pltpu.VMEM((ROWS, WIDTH), F32),
            pltpu.VMEM((ROWS, WIDTH), F32),
            pltpu.VMEM((2,) + shard, F32),
            pltpu.VMEM(shard, F32),
            pltpu.VMEM(shard, F32),
            pltpu.VMEM((LAYERS, WIDTH, WIDTH), BF16),
            pltpu.VMEM((LAYERS, WIDTH, WIDTH), BF16),
            pltpu.VMEM(peers, F32),
            pltpu.VMEM(peers, F32),
            pltpu.VMEM(peers, F32),
            pltpu.VMEM(peers, F32),
            pltpu.VMEM(peers, F32),
            pltpu.VMEM((LAYERS, slots, WIDTH), BF16),
            pltpu.VMEM((LAYERS, slots, WIDTH), BF16),
            pltpu.VMEM((LAYERS - 1, slots, WIDTH), F32),
            pltpu.VMEM((2,) + shard, F32),
            pltpu.VMEM(shard, F32),
            pltpu.VMEM((1, ROWS), jnp.int32),
            pltpu.VMEM((ROWS, 128), jnp.int32),
            pltpu.VMEM(shard, F32),
            pltpu.VMEM(shard, F32),
            pltpu.VMEM(shard, F32),
            pltpu.SemaphoreType.DMA((5,)),
            pltpu.SemaphoreType.DMA((3,)),
            pltpu.SemaphoreType.DMA((3,)),
            pltpu.SemaphoreType.DMA((3, GROUPS)),
            pltpu.SemaphoreType.DMA((2,)),
            pltpu.SemaphoreType.DMA((2,)),
        ],
        compiler_params=pltpu.CompilerParams(
            collective_id=0, has_side_effects=True, vmem_limit_bytes=60 * 2**20
        ),
        cost_estimate=pl.CostEstimate(flops=flops, bytes_accessed=2**23, transcendentals=slots * WIDTH * 6),
    )(
        routes.reshape(1, ROWS),
        samples,
        cotangent,
        weights[:, 0],
        moment_one[:, 0],
        moment_two[:, 0],
    )
    return outputs, new_w[:, None], new_one[:, None], new_two[:, None]


def solution(mesh):
    rows = P(("expert", "replica"), None)
    state = P(None, "expert", "replica", None)
    return jax.shard_map(
        on_device,
        mesh=mesh,
        in_specs=(rows, rows, rows, state, state, state),
        out_specs=(rows, state, state, state),
        check_vma=False,
    )
```

profile of v0, /device:TPU:9, one launch (start us, length us, event | category | flops | bytes accessed | tf_op | source)
XLA Modules:
  0.0 103.9 jit_solution(17443837582390302279)
XLA Ops:
  0.6 97.0 %shard_map.93 = (f32[1024,256]{1,0:T(8,128)}, f32[7,128,256]{2,1,0:T(8,128)}, f32[7,128,256]{2,1,0:T(8,128)}, f32[7,128,256]{2,1,0:T(8,128)}) custom-call(s32[1,1024]{1,0:T(1,128)} %bitcast.19, f32[1024,256]{1,0:T(8,128)} %samples.1, f32[1024,256]{1,0:T(8,128)} %cotangent.1, f32[7,128,256]{2,1,0:T(8,128)} %bitcast.16, f32[7,128,256]{2,1,0:T(8,128)} %bitcast.17, ...), custom_call_target="tpu_custom_call" | custom-call | flops 16106127360 | bytes 8388608 | tf_op jit(solution)/shard_map/pallas_call | solution.py:286
  97.6 0.0 copy-start.2
  97.6 2.3 %copy.17 = f32[1024,256]{1,0:T(8,128)} copy(f32[1024,256]{1,0:T(8,128)} %get-tuple-element.20) | data formatting | bytes 2097152
  100.0 0.0 copy-done.2
  100.0 0.0 copy-start.1
  100.0 0.9 copy.18
  100.9 0.6 copy-done.1
  101.5 0.0 copy-start
  101.5 0.9 copy.19
  102.4 0.6 copy-done
  103.0 0.9 copy.20
Async XLA Ops:
  97.6 2.4 %copy-start.2 = (f32[7,128,256]{2,1,0:T(8,128)S(1)}, f32[7,128,256]{2,1,0:T(8,128)}, u32[]{:S(2)}) copy-start(f32[7,128,256]{2,1,0:T(8,128)} %get-tuple-element.9) | copy-start | bytes 2752516
  100.0 1.5 %copy-start.1 = (f32[7,128,256]{2,1,0:T(8,128)S(1)}, f32[7,128,256]{2,1,0:T(8,128)}, u32[]{:S(2)}) copy-start(f32[7,128,256]{2,1,0:T(8,128)} %get-tuple-element.10) | copy-start | bytes 2752516
  101.5 1.5 %copy-start = (f32[7,128,256]{2,1,0:T(8,128)S(1)}, f32[7,128,256]{2,1,0:T(8,128)}, u32[]{:S(2)}) copy-start(f32[7,128,256]{2,1,0:T(8,128)} %get-tuple-element.11) | copy-start | bytes 2752516
where the time goes:
time: 104 us
  Pallas kernels  97 us (93%)
  local copies, waits for them, and re-layouts  6.29 us (6%)
    pallas_call x1, Pallas kernels, on_device(): pl.pallas_call(kernel, out_shape=(jax.ShapeDtypeStruct((ROWS, WIDTH), F32...  97 us
    unnamed x10, local copies, waits for them, and re-layouts  6.29 us

commit v1 on v0

--- a/solution.py
+++ b/solution.py
@@ -18,9 +18,12 @@
 ROWS = 1024
 LAYERS = 7
 HALF = WIDTH // 2
-PER = 8
+PER = 16
 GROUPS = PEERS // PER
 TILE = PER * CAP
+PACK = 8
+PACKS = PEERS // PACK
+PACK_TILE = PACK * CAP
 STRIDE = 37
 
 
@@ -58,8 +61,8 @@
     return z * (SIDE * SIDE) + y * SIDE + x
 
 
-def wanted(me, group, shape, axis):
-    j = lax.broadcasted_iota(jnp.int32, shape, axis) + group * TILE
+def wanted(me, start, shape, axis):
+    j = lax.broadcasted_iota(jnp.int32, shape, axis) + start
     k = lax.shift_right_logical(j, 5)
     off = (k * STRIDE) & (PEERS - 1)
     x = (me + off) & 3
@@ -71,8 +74,8 @@
 def kernel(
     routes, samples, cotangent, weights, one, two,
     outputs, new_w, new_one, new_two,
-    sv, cv, wf, m1, m2, wh, wl, sp, cp, arr, arc, ret, ah, al, slope, grads, got, slot, slot_t, o_w, o_1, o_2,
-    in_sem, out_sem, send_sem, recv_sem, w_sem, g_sem,
+    sv, cv, wf, m1, m2, wh, wl, sp, cp, arr, arc, ret, ah, al, slope, grads, got, slot, slot_t, place,
+    in_sem, send_sem, recv_sem, w_sem, g_sem,
 ):
     me = lax.axis_index("expert")
     rep = lax.axis_index("replica")
@@ -110,39 +113,38 @@
         base = base + jnp.sum(hot, axis=1, keepdims=True)
         slot[:, b * 256 : (b + 1) * 256] = part * CAP + rank.astype(jnp.int32)
 
-    def remote(phase, src, dst, k, g, to):
+    def remote(phase, src, dst, k, to):
         return pltpu.make_async_remote_copy(
-            src_ref=src, dst_ref=dst, send_sem=send_sem.at[phase], recv_sem=recv_sem.at[phase, g],
+            src_ref=src, dst_ref=dst, send_sem=send_sem.at[phase], recv_sem=recv_sem.at[phase, k // PER],
             device_id={"expert": to}, device_id_type=MESH,
         )
 
-    def send_group(phase, src, dst, g, where):
-        @pl.when(g == 0)
+    def send_range(phase, src, dst, start, count, where):
+        @pl.when(start == 0)
         def _():
             pltpu.make_async_copy(src.at[0], dst.at[0], recv_sem.at[phase, 0]).start()
 
-        @pl.when(g > 0)
+        @pl.when(start > 0)
         def _():
-            k = g * PER
-            remote(phase, src.at[k], dst.at[k], k, g, where(me, k)).start()
+            remote(phase, src.at[start], dst.at[start], start, where(me, start)).start()
 
         def one_send(i, carry):
-            k = g * PER + i
-            remote(phase, src.at[k], dst.at[k], k, g, where(me, k)).start()
+            k = start + i
+            remote(phase, src.at[k], dst.at[k], k, where(me, k)).start()
             return carry
 
-        lax.fori_loop(1, PER, one_send, 0)
+        lax.fori_loop(1, count, one_send, 0)
 
     def wait_group(phase, dst, g):
         block = dst.at[pl.ds(g * PER, PER)]
-        remote(phase, block, block, 0, g, me).wait_recv()
+        remote(phase, block, block, g * PER, me).wait_recv()
 
     def pack_group(high, low, dst, g):
-        want = wanted(me, g, (TILE, 128), 0)
+        want = wanted(me, g * PACK_TILE, (PACK_TILE, 128), 0)
         want = jnp.concatenate([want] * (ROWS // 128), axis=1)
         hot = (want == slot[...]).astype(F32).astype(BF16)
         packed = mm(hot, high) + mm(hot, low)
-        dst[pl.ds(g * PER, PER)] = packed.reshape(PER, CAP, WIDTH)
+        dst[pl.ds(g * PACK, PACK)] = packed.reshape(PACK, CAP, WIDTH)
 
     loads[0].wait()
     s_high, s_low = split(sv[...])
@@ -156,22 +158,35 @@
 
     def pack_samples(g, carry):
         pack_group(s_high, s_low, sp, g)
-        send_group(0, sp, arr, g, peer)
-        return carry
-
-    lax.fori_loop(0, GROUPS, pack_samples, 0)
+        send_range(0, sp, arr, g * PACK, PACK, peer)
+        return carry
+
+    lax.fori_loop(0, PACKS, pack_samples, 0)
 
     loads[2].wait()
     c_high, c_low = split(cv[...])
 
     def pack_cotangent(g, carry):
         pack_group(c_high, c_low, cp, g)
-        send_group(1, cp, arc, g, peer)
-        return carry
-
-    lax.fori_loop(0, GROUPS, pack_cotangent, 0)
+        send_range(1, cp, arc, g * PACK, PACK, peer)
+        return carry
+
+    lax.fori_loop(0, PACKS, pack_cotangent, 0)
 
     slot_t[...] = jnp.transpose(jnp.broadcast_to(slot[...], (128, ROWS)))
+
+    def spread_rows(g, carry):
+        want = wanted(me, g * TILE, (8, TILE), 1)[:1]
+
+        def some_rows(i, carry):
+            rows = pl.ds(i * 256, 256)
+            mine = jnp.concatenate([slot_t[rows]] * (TILE // 128), axis=1)
+            place[g, rows] = (mine == want).astype(F32).astype(BF16)
+            return carry
+
+        return lax.fori_loop(0, ROWS // 256, some_rows, carry)
+
+    lax.fori_loop(0, GROUPS, spread_rows, 0)
 
     weight_copy.wait()
 
@@ -198,14 +213,14 @@
             if layer < LAYERS - 1:
                 sigma = jax.nn.sigmoid(pre)
                 hidden = pre * sigma
-                slope[layer, rows] = sigma * (1.0 + pre * (1.0 - sigma))
+                slope[layer, rows] = sigma + hidden * (1.0 - sigma)
         arr[pl.ds(g * PER, PER)] = pre.reshape(PER, CAP, WIDTH)
-        send_group(2, arr, ret, g, peer_back)
         return carry
 
     lax.fori_loop(0, GROUPS, forward, 0)
 
     def backward(g, carry):
+        send_range(2, arr, ret, g * PER, PER, peer_back)
         wait_group(1, arc, g)
         rows = pl.ds(g * TILE, TILE)
         delta = arc[pl.ds(g * PER, PER)].reshape(TILE, WIDTH)
@@ -220,13 +235,29 @@
                 delta = back * slope[layer - 1, rows]
         return carry
 
-    lax.fori_loop(0, GROUPS, backward, 0)
+    def unpack(g, first):
+        wait_group(2, ret, g)
+        high, low = split(ret[pl.ds(g * PER, PER)].reshape(TILE, WIDTH))
+
+        def some_rows(i, carry):
+            rows = pl.ds(i * 256, 256)
+            hot = place[g, rows]
+            found = mm(hot, high) + mm(hot, low)
+            outputs[rows] = found if first else outputs[rows] + found
+            return carry
+
+        lax.fori_loop(0, ROWS // 256, some_rows, 0)
+
+    lax.fori_loop(0, GROUPS - 1, backward, 0)
+    unpack(0, True)
+    backward(GROUPS - 1, 0)
 
     grad_copy = pltpu.make_async_remote_copy(
         src_ref=grads.at[other], dst_ref=got, send_sem=g_sem.at[0], recv_sem=g_sem.at[1],
         device_id={"replica": other}, device_id_type=MESH,
     )
     grad_copy.start()
+    unpack(1, False)
     loads[3].wait()
     loads[4].wait()
     grad_copy.wait()
@@ -235,44 +266,29 @@
         grad = grads[rep, layer] + got[layer]
         first = 0.9 * m1[layer] + 0.1 * grad
         second = 0.999 * m2[layer] + 0.001 * grad * grad
-        o_1[layer] = first
-        o_2[layer] = second
-        o_w[layer] = wf[rep, layer] - 0.01 * (first / CORR_ONE) / (jnp.sqrt(second / CORR_TWO) + 1e-08)
+        new_one[layer] = first
+        new_two[layer] = second
+        new_w[layer] = wf[rep, layer] - 0.01 * (first / CORR_ONE) / (jnp.sqrt(second / CORR_TWO) + 1e-08)
         return carry
 
     lax.fori_loop(0, LAYERS, adam, 0)
-    stores = [
-        pltpu.make_async_copy(src, dst, out_sem.at[i])
-        for i, (src, dst) in enumerate(((o_w, new_w), (o_1, new_one), (o_2, new_two)))
-    ]
-    for store in stores:
-        store.start()
-
-    outputs[...] = jnp.zeros((ROWS, WIDTH), F32)
-
-    def unpack(g, carry):
-        wait_group(2, ret, g)
-        high, low = split(ret[pl.ds(g * PER, PER)].reshape(TILE, WIDTH))
-        want = wanted(me, g, (8, TILE), 1)[:1]
-
-        def some_rows(i, carry):
-            rows = pl.ds(i * 256, 256)
-            mine = slot_t[rows]
-            mine = jnp.concatenate([mine, mine], axis=1)
-            hot = (mine == want).astype(F32).astype(BF16)
-            outputs[rows] += mm(hot, high) + mm(hot, low)
-            return carry
-
-        lax.fori_loop(0, ROWS // 256, some_rows, 0)
-        return carry
-
-    lax.fori_loop(0, GROUPS, unpack, 0)
-
-    for store in stores:
-        store.wait()
+    for g in range(2, GROUPS):
+        unpack(g, False)
+
     for phase, src in enumerate((sp, cp, arr)):
         block = src.at[pl.ds(1, PEERS - 1)]
-        remote(phase, block, block, 0, 0, me).wait_send()
+        remote(phase, block, block, 0, me).wait_send()
+
+
+def store_kernel(a, b, c, d, out_a, out_b, out_c, out_d, sem):
+    copies = [
+        pltpu.make_async_copy(src, dst, sem.at[i])
+        for i, (src, dst) in enumerate(((a, out_a), (b, out_b), (c, out_c), (d, out_d)))
+    ]
+    for copy in copies:
+        copy.start()
+    for copy in copies:
+        copy.wait()
 
 
 def on_device(samples, routes, cotangent, weights, moment_one, moment_two):
@@ -283,11 +299,11 @@
     peers = (PEERS, CAP, WIDTH)
     slots = PEERS * CAP
     flops = 2 * slots * WIDTH * WIDTH * 60
-    outputs, new_w, new_one, new_two = pl.pallas_call(
+    held = pl.pallas_call(
         kernel,
-        out_shape=(jax.ShapeDtypeStruct((ROWS, WIDTH), F32), state, state, state),
+        out_shape=(pltpu.VMEM((ROWS, WIDTH), F32),) + (pltpu.VMEM(shard, F32),) * 3,
         in_specs=[vmem] + [hbm] * 5,
-        out_specs=(vmem, hbm, hbm, hbm),
+        out_specs=(vmem,) * 4,
         scratch_shapes=[
             pltpu.VMEM((ROWS, WIDTH), F32),
             pltpu.VMEM((ROWS, WIDTH), F32),
@@ -308,18 +324,15 @@
             pltpu.VMEM(shard, F32),
             pltpu.VMEM((1, ROWS), jnp.int32),
             pltpu.VMEM((ROWS, 128), jnp.int32),
-            pltpu.VMEM(shard, F32),
-            pltpu.VMEM(shard, F32),
-            pltpu.VMEM(shard, F32),
+            pltpu.VMEM((GROUPS, ROWS, TILE), BF16),
             pltpu.SemaphoreType.DMA((5,)),
-            pltpu.SemaphoreType.DMA((3,)),
             pltpu.SemaphoreType.DMA((3,)),
             pltpu.SemaphoreType.DMA((3, GROUPS)),
             pltpu.SemaphoreType.DMA((2,)),
             pltpu.SemaphoreType.DMA((2,)),
         ],
         compiler_params=pltpu.CompilerParams(
-            collective_id=0, has_side_effects=True, vmem_limit_bytes=60 * 2**20
+            collective_id=0, has_side_effects=True, vmem_limit_bytes=56 * 2**20
         ),
         cost_estimate=pl.CostEstimate(flops=flops, bytes_accessed=2**23, transcendentals=slots * WIDTH * 6),
     )(
@@ -330,6 +343,14 @@
         moment_one[:, 0],
         moment_two[:, 0],
     )
+    outputs, new_w, new_one, new_two = pl.pallas_call(
+        store_kernel,
+        out_shape=(jax.ShapeDtypeStruct((ROWS, WIDTH), F32), state, state, state),
+        in_specs=[vmem] * 4,
+        out_specs=(hbm,) * 4,
+        scratch_shapes=[pltpu.SemaphoreType.DMA((4,))],
+        compiler_params=pltpu.CompilerParams(vmem_limit_bytes=2**22),
+    )(*(pltpu.with_memory_space_constraint(x, pltpu.VMEM) for x in held))
     return outputs, new_w[:, None], new_one[:, None], new_two[:, None]
 
 

time: 104 us -> 87.7 us (0.84)
  the two profiles are of different devices: /device:TPU:9 before, /device:TPU:0 now
where the time goes in v1:
time: 87.7 us; the launch traced here: 86.5 us
  Pallas kernels  85.9 us (98%)
    pallas_call x1, Pallas kernels, on_device(): pl.pallas_call(kernel, out_shape=(pltpu.VMEM((ROWS, WIDTH), F32),) + (plt...  84 us
    pallas_call x1, Pallas kernels, on_device(): pl.pallas_call(store_kernel, out_shape=(jax.ShapeDtypeStruct((ROWS, WIDTH...  1.91 us

profile of v1, /device:TPU:0, one launch (start us, length us, event | category | flops | bytes accessed | tf_op | source)
XLA Modules:
  0.0 86.5 jit_solution(15251844631787870758)
XLA Ops:
  0.6 84.0 %shard_map.93 = (f32[1024,256]{1,0:T(8,128)S(1)}, f32[7,128,256]{2,1,0:T(8,128)S(1)}, f32[7,128,256]{2,1,0:T(8,128)S(1)}, f32[7,128,256]{2,1,0:T(8,128)S(1)}) custom-call(s32[1,1024]{1,0:T(1,128)} %bitcast.19, f32[1024,256]{1,0:T(8,128)} %samples.1, f32[1024,256]{1,0:T(8,128)} %cotangent.1, f32[7,128,256]{2,1,0:T(8,128)} %bitcast.13, ...), custom_call_target="tpu_custom_call" | custom-call | flops 16106127360 | bytes 8388608 | tf_op jit(solution)/shard_map/pallas_call | solution.py:302
  84.6 1.9 %shard_map.94 = (f32[1024,256]{1,0:T(8,128)}, f32[7,128,256]{2,1,0:T(8,128)}, f32[7,128,256]{2,1,0:T(8,128)}, f32[7,128,256]{2,1,0:T(8,128)}) custom-call(f32[1024,256]{1,0:T(8,128)S(1)} %get-tuple-element.12.a, f32[7,128,256]{2,1,0:T(8,128)S(1)} %get-tuple-element.13.b, f32[7,128,256]{2,1,0:T(8,128)S(1)} %get-tuple-element.14.c, ...), custom_call_target="tpu_custom_call" | custom-call | tf_op jit(solution)/shard_map/pallas_call | solution.py:346

commit v2 on v1

--- a/solution.py
+++ b/solution.py
@@ -24,7 +24,7 @@
 PACK = 8
 PACKS = PEERS // PACK
 PACK_TILE = PACK * CAP
-STRIDE = 37
+STRIDE = 27
 
 
 def split(value):
@@ -46,18 +46,18 @@
 
 
 def peer(me, k):
-    off = (k * STRIDE) % PEERS
-    x = (me + off) % SIDE
-    y = (me // SIDE + off // SIDE) % SIDE
-    z = (me // (SIDE * SIDE) + off // (SIDE * SIDE)) % SIDE
+    off = lax.rem(k * STRIDE, PEERS)
+    x = lax.rem(me + off, SIDE)
+    y = lax.rem(lax.div(me, SIDE) + lax.div(off, SIDE), SIDE)
+    z = lax.rem(lax.div(me, SIDE * SIDE) + lax.div(off, SIDE * SIDE), SIDE)
     return z * (SIDE * SIDE) + y * SIDE + x
 
 
 def peer_back(me, k):
-    off = (k * STRIDE) % PEERS
-    x = (me + SIDE - off % SIDE) % SIDE
-    y = (me // SIDE + SIDE - (off // SIDE) % SIDE) % SIDE
-    z = (me // (SIDE * SIDE) + SIDE - off // (SIDE * SIDE)) % SIDE
+    off = lax.rem(k * STRIDE, PEERS)
+    x = lax.rem(me + SIDE - lax.rem(off, SIDE), SIDE)
+    y = lax.rem(lax.div(me, SIDE) + SIDE - lax.rem(lax.div(off, SIDE), SIDE), SIDE)
+    z = lax.rem(lax.div(me, SIDE * SIDE) + SIDE - lax.div(off, SIDE * SIDE), SIDE)
     return z * (SIDE * SIDE) + y * SIDE + x
 
 
@@ -73,13 +73,26 @@
 
 def kernel(
     routes, samples, cotangent, weights, one, two,
-    outputs, new_w, new_one, new_two,
-    sv, cv, wf, m1, m2, wh, wl, sp, cp, arr, arc, ret, ah, al, slope, grads, got, slot, slot_t, place,
+    ret, place, outputs, new_w, new_one, new_two,
+    sv, cv, wf, m1, m2, wh, wl, sp, cp, arr, arc, ah, al, slope, grads, got, slot, slot_t,
     in_sem, send_sem, recv_sem, w_sem, g_sem,
 ):
     me = lax.axis_index("expert")
     rep = lax.axis_index("replica")
     other = 1 - rep
+
+    barrier = pltpu.get_barrier_semaphore()
+    at_x = lax.rem(me, SIDE)
+    at_y = lax.rem(lax.div(me, SIDE), SIDE)
+    at_z = lax.div(me, SIDE * SIDE)
+    xs, ys, zs = (
+        [at] + [lax.rem(at + step, SIDE) for step in range(1, SIDE)] for at in (at_x, at_y, at_z)
+    )
+    for off in range(PEERS - 1, 0, -1):
+        z, y, x = zs[off // 16], ys[off // 4 % 4], xs[off % 4]
+        to = z * (SIDE * SIDE) + y * SIDE + x
+        pl.semaphore_signal(barrier, inc=1, device_id={"expert": to}, device_id_type=MESH)
+    pl.semaphore_signal(barrier, inc=1, device_id={"replica": other}, device_id_type=MESH)
 
     loads = [
         pltpu.make_async_copy(src, dst, in_sem.at[i])
@@ -89,15 +102,6 @@
     ]
     for load in loads:
         load.start()
-
-    barrier = pltpu.get_barrier_semaphore()
-
-    def greet(k, carry):
-        pl.semaphore_signal(barrier, inc=1, device_id={"expert": peer_back(me, k)}, device_id_type=MESH)
-        return carry
-
-    lax.fori_loop(1, PEERS, greet, 0)
-    pl.semaphore_signal(barrier, inc=1, device_id={"replica": other}, device_id_type=MESH)
 
     route = routes[...]
     earlier = (
@@ -148,8 +152,10 @@
 
     loads[0].wait()
     s_high, s_low = split(sv[...])
+    pack_group(s_high, s_low, sp, 0)
+    pl.semaphore_wait(barrier, PEERS)
+    send_range(0, sp, arr, 0, PACK, peer)
     loads[1].wait()
-    pl.semaphore_wait(barrier, PEERS)
     weight_copy = pltpu.make_async_remote_copy(
         src_ref=wf.at[rep], dst_ref=wf.at[rep], send_sem=w_sem.at[0], recv_sem=w_sem.at[1],
         device_id={"replica": other}, device_id_type=MESH,
@@ -161,7 +167,7 @@
         send_range(0, sp, arr, g * PACK, PACK, peer)
         return carry
 
-    lax.fori_loop(0, PACKS, pack_samples, 0)
+    lax.fori_loop(1, PACKS, pack_samples, 0)
 
     loads[2].wait()
     c_high, c_low = split(cv[...])
@@ -272,21 +278,30 @@
         return carry
 
     lax.fori_loop(0, LAYERS, adam, 0)
-    for g in range(2, GROUPS):
+    for g in range(2, GROUPS - 1):
         unpack(g, False)
+    wait_group(2, ret, GROUPS - 1)
 
     for phase, src in enumerate((sp, cp, arr)):
         block = src.at[pl.ds(1, PEERS - 1)]
         remote(phase, block, block, 0, me).wait_send()
 
 
-def store_kernel(a, b, c, d, out_a, out_b, out_c, out_d, sem):
+def finish(ret, place, partial, w, one, two, outputs, new_w, new_one, new_two, rows_out, sem):
     copies = [
         pltpu.make_async_copy(src, dst, sem.at[i])
-        for i, (src, dst) in enumerate(((a, out_a), (b, out_b), (c, out_c), (d, out_d)))
+        for i, (src, dst) in enumerate(((w, new_w), (one, new_one), (two, new_two)))
     ]
     for copy in copies:
         copy.start()
+    high, low = split(ret[PEERS - PER :].reshape(TILE, WIDTH))
+    part = 256
+    for i in range(ROWS // part):
+        rows = pl.ds(i * part, part)
+        hot = place[GROUPS - 1, rows]
+        rows_out[rows] = partial[rows] + mm(hot, high) + mm(hot, low)
+        copies.append(pltpu.make_async_copy(rows_out.at[rows], outputs.at[rows], sem.at[3 + i]))
+        copies[-1].start()
     for copy in copies:
         copy.wait()
 
@@ -301,9 +316,16 @@
     flops = 2 * slots * WIDTH * WIDTH * 60
     held = pl.pallas_call(
         kernel,
-        out_shape=(pltpu.VMEM((ROWS, WIDTH), F32),) + (pltpu.VMEM(shard, F32),) * 3,
+        out_shape=(
+            pltpu.VMEM(peers, F32),
+            pltpu.VMEM((GROUPS, ROWS, TILE), BF16),
+            pltpu.VMEM((ROWS, WIDTH), F32),
+            pltpu.VMEM(shard, F32),
+            pltpu.VMEM(shard, F32),
+            pltpu.VMEM(shard, F32),
+        ),
         in_specs=[vmem] + [hbm] * 5,
-        out_specs=(vmem,) * 4,
+        out_specs=(vmem,) * 6,
         scratch_shapes=[
             pltpu.VMEM((ROWS, WIDTH), F32),
             pltpu.VMEM((ROWS, WIDTH), F32),
@@ -316,7 +338,6 @@
             pltpu.VMEM(peers, F32),
             pltpu.VMEM(peers, F32),
             pltpu.VMEM(peers, F32),
-            pltpu.VMEM(peers, F32),
             pltpu.VMEM((LAYERS, slots, WIDTH), BF16),
             pltpu.VMEM((LAYERS, slots, WIDTH), BF16),
             pltpu.VMEM((LAYERS - 1, slots, WIDTH), F32),
@@ -324,7 +345,6 @@
             pltpu.VMEM(shard, F32),
             pltpu.VMEM((1, ROWS), jnp.int32),
             pltpu.VMEM((ROWS, 128), jnp.int32),
-            pltpu.VMEM((GROUPS, ROWS, TILE), BF16),
             pltpu.SemaphoreType.DMA((5,)),
             pltpu.SemaphoreType.DMA((3,)),
             pltpu.SemaphoreType.DMA((3, GROUPS)),
@@ -332,7 +352,7 @@
             pltpu.SemaphoreType.DMA((2,)),
         ],
         compiler_params=pltpu.CompilerParams(
-            collective_id=0, has_side_effects=True, vmem_limit_bytes=56 * 2**20
+            collective_id=0, has_side_effects=True, vmem_limit_bytes=50 * 2**20
         ),
         cost_estimate=pl.CostEstimate(flops=flops, bytes_accessed=2**23, transcendentals=slots * WIDTH * 6),
     )(
@@ -344,12 +364,12 @@
         moment_two[:, 0],
     )
     outputs, new_w, new_one, new_two = pl.pallas_call(
-        store_kernel,
+        finish,
         out_shape=(jax.ShapeDtypeStruct((ROWS, WIDTH), F32), state, state, state),
-        in_specs=[vmem] * 4,
+        in_specs=[vmem] * 6,
         out_specs=(hbm,) * 4,
-        scratch_shapes=[pltpu.SemaphoreType.DMA((4,))],
-        compiler_params=pltpu.CompilerParams(vmem_limit_bytes=2**22),
+        scratch_shapes=[pltpu.VMEM((ROWS, WIDTH), F32), pltpu.SemaphoreType.DMA((7,))],
+        compiler_params=pltpu.CompilerParams(vmem_limit_bytes=2**23),
     )(*(pltpu.with_memory_space_constraint(x, pltpu.VMEM) for x in held))
     return outputs, new_w[:, None], new_one[:, None], new_two[:, None]
 

time: 87.7 us -> 83.7 us (0.954)
  Pallas kernels: 85.9 us -> 82.4 us
    pallas_call x2, Pallas kernels: 85.9 us -> 82.4 us  [the longest x1 80.5 us: on_device(): pl.pallas_call(kernel, out_shape=(pltpu.VMEM(peers, F32), pltpu.VMEM((GRO...]
where the time goes in v2:
time: 83.7 us; the launch traced here: 83 us
  Pallas kernels  82.4 us (98%)
    pallas_call x1, Pallas kernels, on_device(): pl.pallas_call(kernel, out_shape=(pltpu.VMEM(peers, F32), pltpu.VMEM((GRO...  80.5 us
    pallas_call x1, Pallas kernels, on_device(): pl.pallas_call(finish, out_shape=(jax.ShapeDtypeStruct((ROWS, WIDTH), F32...  1.93 us

profile of v2, /device:TPU:0, one launch (start us, length us, event | category | flops | bytes accessed | tf_op | source)
XLA Modules:
  0.0 83.0 jit_solution(13714589713740323438)
XLA Ops:
  0.6 80.5 %shard_map.93 = (f32[64,32,256]{2,1,0:T(8,128)S(1)}, bf16[4,1024,512]{2,1,0:T(8,128)(2,1)S(1)}, f32[1024,256]{1,0:T(8,128)S(1)}, f32[7,128,256]{2,1,0:T(8,128)S(...) custom-call(s32[1,1024]{1,0:T(1,128)} %bitcast.19, f32[1024,256]{1,0:T(8,128)} %samples.1, ...), custom_call_target="tpu_custom_call" | custom-call | flops 16106127360 | bytes 8388608 | tf_op jit(solution)/shard_map/pallas_call | solution.py:317
  81.1 1.9 %shard_map.94 = (f32[1024,256]{1,0:T(8,128)}, f32[7,128,256]{2,1,0:T(8,128)}, f32[7,128,256]{2,1,0:T(8,128)}, f32[7,128,256]{2,1,0:T(8,128)}) custom-call(f32[64,32,256]{2,1,0:T(8,128)S(1)} %get-tuple-element.14.ret, bf16[4,1024,512]{2,1,0:T(8,128)(2,1)S(1)} %get-tuple-element.15.place, f32[1024,256]{1,0:T(8,128)S(1)} %get-tuple-element.16.partial, ...), custom_call_target="tpu_custom_call" | custom-call | tf_op jit(solution)/shard_map/pallas_call | solution.py:366

commit v3 on v2

--- a/solution.py
+++ b/solution.py
@@ -74,12 +74,21 @@
 def kernel(
     routes, samples, cotangent, weights, one, two,
     ret, place, outputs, new_w, new_one, new_two,
-    sv, cv, wf, m1, m2, wh, wl, sp, cp, arr, arc, ah, al, slope, grads, got, slot, slot_t,
+    rv, sv, cv, wf, m1, m2, wh, wl, sp, cp, arr, arc, ah, al, slope, grads, got, slot, slot_t,
     in_sem, send_sem, recv_sem, w_sem, g_sem,
 ):
     me = lax.axis_index("expert")
     rep = lax.axis_index("replica")
     other = 1 - rep
+
+    loads = [
+        pltpu.make_async_copy(src, dst, in_sem.at[i])
+        for i, (src, dst) in enumerate(
+            ((samples, sv), (weights, wf.at[rep]), (cotangent, cv), (one, m1), (two, m2), (routes, rv))
+        )
+    ]
+    loads[5].start()
+    loads[0].start()
 
     barrier = pltpu.get_barrier_semaphore()
     at_x = lax.rem(me, SIDE)
@@ -94,16 +103,11 @@
         pl.semaphore_signal(barrier, inc=1, device_id={"expert": to}, device_id_type=MESH)
     pl.semaphore_signal(barrier, inc=1, device_id={"replica": other}, device_id_type=MESH)
 
-    loads = [
-        pltpu.make_async_copy(src, dst, in_sem.at[i])
-        for i, (src, dst) in enumerate(
-            ((samples, sv), (weights, wf.at[rep]), (cotangent, cv), (one, m1), (two, m2))
-        )
-    ]
-    for load in loads:
+    for load in loads[1:5]:
         load.start()
 
-    route = routes[...]
+    loads[5].wait()
+    route = rv[...]
     earlier = (
         lax.broadcasted_iota(jnp.int32, (256, 256), 0) < lax.broadcasted_iota(jnp.int32, (256, 256), 1)
     ).astype(F32).astype(BF16)
@@ -324,9 +328,10 @@
             pltpu.VMEM(shard, F32),
             pltpu.VMEM(shard, F32),
         ),
-        in_specs=[vmem] + [hbm] * 5,
+        in_specs=[hbm] * 6,
         out_specs=(vmem,) * 6,
         scratch_shapes=[
+            pltpu.VMEM((1, ROWS), jnp.int32),
             pltpu.VMEM((ROWS, WIDTH), F32),
             pltpu.VMEM((ROWS, WIDTH), F32),
             pltpu.VMEM((2,) + shard, F32),
@@ -345,7 +350,7 @@
             pltpu.VMEM(shard, F32),
             pltpu.VMEM((1, ROWS), jnp.int32),
             pltpu.VMEM((ROWS, 128), jnp.int32),
-            pltpu.SemaphoreType.DMA((5,)),
+            pltpu.SemaphoreType.DMA((6,)),
             pltpu.SemaphoreType.DMA((3,)),
             pltpu.SemaphoreType.DMA((3, GROUPS)),
             pltpu.SemaphoreType.DMA((2,)),

time: 83.7 us -> 82.5 us (0.986)
  no operation moved by 1% of the time
where the time goes in v3:
time: 82.5 us; the launch traced here: 82.4 us
  Pallas kernels  81.8 us (99%)
    pallas_call x1, Pallas kernels, on_device(): pl.pallas_call(kernel, out_shape=(pltpu.VMEM(peers, F32), pltpu.VMEM((GRO...  79.8 us
    pallas_call x1, Pallas kernels, on_device(): pl.pallas_call(finish, out_shape=(jax.ShapeDtypeStruct((ROWS, WIDTH), F32...  1.93 us

profile of v3, /device:TPU:0, one launch (start us, length us, event | category | flops | bytes accessed | tf_op | source)
XLA Modules:
  0.0 82.4 jit_solution(7236503686166015300)
XLA Ops:
  0.6 79.8 %shard_map.93 = (f32[64,32,256]{2,1,0:T(8,128)S(1)}, bf16[4,1024,512]{2,1,0:T(8,128)(2,1)S(1)}, f32[1024,256]{1,0:T(8,128)S(1)}, f32[7,128,256]{2,1,0:T(8,128)S(...) custom-call(s32[1,1024]{1,0:T(1,128)} %bitcast.19, f32[1024,256]{1,0:T(8,128)} %samples.1, ...), custom_call_target="tpu_custom_call" | custom-call | flops 16106127360 | bytes 8388608 | tf_op jit(solution)/shard_map/pallas_call | solution.py:321
  80.5 1.9 %shard_map.94 = (f32[1024,256]{1,0:T(8,128)}, f32[7,128,256]{2,1,0:T(8,128)}, f32[7,128,256]{2,1,0:T(8,128)}, f32[7,128,256]{2,1,0:T(8,128)}) custom-call(f32[64,32,256]{2,1,0:T(8,128)S(1)} %get-tuple-element.14.ret, bf16[4,1024,512]{2,1,0:T(8,128)(2,1)S(1)} %get-tuple-element.15.place, f32[1024,256]{1,0:T(8,128)S(1)} %get-tuple-element.16.partial, ...), custom_call_target="tpu_custom_call" | custom-call | tf_op jit(solution)/shard_map/pallas_call | solution.py:371

commit v4 on v3

--- a/solution.py
+++ b/solution.py
@@ -103,9 +103,6 @@
         pl.semaphore_signal(barrier, inc=1, device_id={"expert": to}, device_id_type=MESH)
     pl.semaphore_signal(barrier, inc=1, device_id={"replica": other}, device_id_type=MESH)
 
-    for load in loads[1:5]:
-        load.start()
-
     loads[5].wait()
     route = rv[...]
     earlier = (
@@ -159,19 +156,21 @@
     pack_group(s_high, s_low, sp, 0)
     pl.semaphore_wait(barrier, PEERS)
     send_range(0, sp, arr, 0, PACK, peer)
+    for load in loads[1:5]:
+        load.start()
+    def pack_samples(g, carry):
+        pack_group(s_high, s_low, sp, g)
+        send_range(0, sp, arr, g * PACK, PACK, peer)
+        return carry
+
+    lax.fori_loop(1, PACKS, pack_samples, 0)
+
     loads[1].wait()
     weight_copy = pltpu.make_async_remote_copy(
         src_ref=wf.at[rep], dst_ref=wf.at[rep], send_sem=w_sem.at[0], recv_sem=w_sem.at[1],
         device_id={"replica": other}, device_id_type=MESH,
     )
     weight_copy.start()
-
-    def pack_samples(g, carry):
-        pack_group(s_high, s_low, sp, g)
-        send_range(0, sp, arr, g * PACK, PACK, peer)
-        return carry
-
-    lax.fori_loop(1, PACKS, pack_samples, 0)
 
     loads[2].wait()
     c_high, c_low = split(cv[...])
@@ -230,7 +229,6 @@
     lax.fori_loop(0, GROUPS, forward, 0)
 
     def backward(g, carry):
-        send_range(2, arr, ret, g * PER, PER, peer_back)
         wait_group(1, arc, g)
         rows = pl.ds(g * TILE, TILE)
         delta = arc[pl.ds(g * PER, PER)].reshape(TILE, WIDTH)
@@ -258,7 +256,12 @@
 
         lax.fori_loop(0, ROWS // 256, some_rows, 0)
 
-    lax.fori_loop(0, GROUPS - 1, backward, 0)
+    def send_and_backward(g, carry):
+        send_range(2, arr, ret, g * PER, PER, peer_back)
+        return backward(g, carry)
+
+    lax.fori_loop(0, GROUPS - 1, send_and_backward, 0)
+    send_range(2, arr, ret, (GROUPS - 1) * PER, PER, peer_back)
     unpack(0, True)
     backward(GROUPS - 1, 0)
 

time: 82.5 us -> 82.5 us (level)
  no operation moved by 1% of the time
where the time goes in v4:
time: 82.5 us; the launch traced here: 82.4 us
  Pallas kernels  81.8 us (99%)
    pallas_call x1, Pallas kernels, on_device(): pl.pallas_call(kernel, out_shape=(pltpu.VMEM(peers, F32), pltpu.VMEM((GRO...  79.8 us
    pallas_call x1, Pallas kernels, on_device(): pl.pallas_call(finish, out_shape=(jax.ShapeDtypeStruct((ROWS, WIDTH), F32...  1.93 us

profile of v4, /device:TPU:0, one launch (start us, length us, event | category | flops | bytes accessed | tf_op | source)
XLA Modules:
  0.0 82.4 jit_solution(2587350379668267244)
XLA Ops:
  0.6 79.8 %shard_map.93 = (f32[64,32,256]{2,1,0:T(8,128)S(1)}, bf16[4,1024,512]{2,1,0:T(8,128)(2,1)S(1)}, f32[1024,256]{1,0:T(8,128)S(1)}, f32[7,128,256]{2,1,0:T(8,128)S(...) custom-call(s32[1,1024]{1,0:T(1,128)} %bitcast.19, f32[1024,256]{1,0:T(8,128)} %samples.1, ...), custom_call_target="tpu_custom_call" | custom-call | flops 16106127360 | bytes 8388608 | tf_op jit(solution)/shard_map/pallas_call | solution.py:324
  80.5 1.9 %shard_map.94 = (f32[1024,256]{1,0:T(8,128)}, f32[7,128,256]{2,1,0:T(8,128)}, f32[7,128,256]{2,1,0:T(8,128)}, f32[7,128,256]{2,1,0:T(8,128)}) custom-call(f32[64,32,256]{2,1,0:T(8,128)S(1)} %get-tuple-element.14.ret, bf16[4,1024,512]{2,1,0:T(8,128)(2,1)S(1)} %get-tuple-element.15.place, f32[1024,256]{1,0:T(8,128)S(1)} %get-tuple-element.16.partial, ...), custom_call_target="tpu_custom_call" | custom-call | tf_op jit(solution)/shard_map/pallas_call | solution.py:374

commit v5 on v4

--- a/solution.py
+++ b/solution.py
@@ -24,7 +24,7 @@
 PACK = 8
 PACKS = PEERS // PACK
 PACK_TILE = PACK * CAP
-STRIDE = 27
+STRIDE = 19
 
 
 def split(value):
@@ -45,29 +45,21 @@
     return lax.dot_general(a, b, (((0,), (0,)), ((), ())), preferred_element_type=F32)
 
 
-def peer(me, k):
+def peer(me, k, turn):
     off = lax.rem(k * STRIDE, PEERS)
-    x = lax.rem(me + off, SIDE)
-    y = lax.rem(lax.div(me, SIDE) + lax.div(off, SIDE), SIDE)
-    z = lax.rem(lax.div(me, SIDE * SIDE) + lax.div(off, SIDE * SIDE), SIDE)
+    x = lax.rem(me + off * turn, SIDE)
+    y = lax.rem(lax.div(me, SIDE) + lax.div(off, SIDE) * turn, SIDE)
+    z = lax.rem(lax.div(me, SIDE * SIDE) + lax.div(off, SIDE * SIDE) * turn, SIDE)
     return z * (SIDE * SIDE) + y * SIDE + x
 
 
-def peer_back(me, k):
-    off = lax.rem(k * STRIDE, PEERS)
-    x = lax.rem(me + SIDE - lax.rem(off, SIDE), SIDE)
-    y = lax.rem(lax.div(me, SIDE) + SIDE - lax.rem(lax.div(off, SIDE), SIDE), SIDE)
-    z = lax.rem(lax.div(me, SIDE * SIDE) + SIDE - lax.div(off, SIDE * SIDE), SIDE)
-    return z * (SIDE * SIDE) + y * SIDE + x
-
-
-def wanted(me, start, shape, axis):
+def wanted(me, turn, start, shape, axis):
     j = lax.broadcasted_iota(jnp.int32, shape, axis) + start
     k = lax.shift_right_logical(j, 5)
     off = (k * STRIDE) & (PEERS - 1)
-    x = (me + off) & 3
-    y = (lax.shift_right_logical(off, 2) + me // SIDE) & 3
-    z = (lax.shift_right_logical(off, 4) + me // (SIDE * SIDE)) & 3
+    x = (me + off * turn) & 3
+    y = (me // SIDE + lax.shift_right_logical(off, 2) * turn) & 3
+    z = (me // (SIDE * SIDE) + lax.shift_right_logical(off, 4) * turn) & 3
     return (z * 16 + y * 4 + x) * CAP + (j & (CAP - 1))
 
 
@@ -80,6 +72,8 @@
     me = lax.axis_index("expert")
     rep = lax.axis_index("replica")
     other = 1 - rep
+    turn = 1 + 2 * rep
+    turn_back = 3 - 2 * rep
 
     loads = [
         pltpu.make_async_copy(src, dst, in_sem.at[i])
@@ -131,11 +125,11 @@
 
         @pl.when(start > 0)
         def _():
-            remote(phase, src.at[start], dst.at[start], start, where(me, start)).start()
+            remote(phase, src.at[start], dst.at[start], start, peer(me, start, where)).start()
 
         def one_send(i, carry):
             k = start + i
-            remote(phase, src.at[k], dst.at[k], k, where(me, k)).start()
+            remote(phase, src.at[k], dst.at[k], k, peer(me, k, where)).start()
             return carry
 
         lax.fori_loop(1, count, one_send, 0)
@@ -145,7 +139,7 @@
         remote(phase, block, block, g * PER, me).wait_recv()
 
     def pack_group(high, low, dst, g):
-        want = wanted(me, g * PACK_TILE, (PACK_TILE, 128), 0)
+        want = wanted(me, turn, g * PACK_TILE, (PACK_TILE, 128), 0)
         want = jnp.concatenate([want] * (ROWS // 128), axis=1)
         hot = (want == slot[...]).astype(F32).astype(BF16)
         packed = mm(hot, high) + mm(hot, low)
@@ -155,12 +149,12 @@
     s_high, s_low = split(sv[...])
     pack_group(s_high, s_low, sp, 0)
     pl.semaphore_wait(barrier, PEERS)
-    send_range(0, sp, arr, 0, PACK, peer)
+    send_range(0, sp, arr, 0, PACK, turn)
     for load in loads[1:5]:
         load.start()
     def pack_samples(g, carry):
         pack_group(s_high, s_low, sp, g)
-        send_range(0, sp, arr, g * PACK, PACK, peer)
+        send_range(0, sp, arr, g * PACK, PACK, turn)
         return carry
 
     lax.fori_loop(1, PACKS, pack_samples, 0)
@@ -177,7 +171,7 @@
 
     def pack_cotangent(g, carry):
         pack_group(c_high, c_low, cp, g)
-        send_range(1, cp, arc, g * PACK, PACK, peer)
+        send_range(1, cp, arc, g * PACK, PACK, turn)
         return carry
 
     lax.fori_loop(0, PACKS, pack_cotangent, 0)
@@ -185,7 +179,7 @@
     slot_t[...] = jnp.transpose(jnp.broadcast_to(slot[...], (128, ROWS)))
 
     def spread_rows(g, carry):
-        want = wanted(me, g * TILE, (8, TILE), 1)[:1]
+        want = wanted(me, turn, g * TILE, (8, TILE), 1)[:1]
 
         def some_rows(i, carry):
             rows = pl.ds(i * 256, 256)
@@ -257,11 +251,11 @@
         lax.fori_loop(0, ROWS // 256, some_rows, 0)
 
     def send_and_backward(g, carry):
-        send_range(2, arr, ret, g * PER, PER, peer_back)
+        send_range(2, arr, ret, g * PER, PER, turn_back)
         return backward(g, carry)
 
     lax.fori_loop(0, GROUPS - 1, send_and_backward, 0)
-    send_range(2, arr, ret, (GROUPS - 1) * PER, PER, peer_back)
+    send_range(2, arr, ret, (GROUPS - 1) * PER, PER, turn_back)
     unpack(0, True)
     backward(GROUPS - 1, 0)
 

time: 82.5 us -> 82.5 us (level)
  no operation moved by 1% of the time
where the time goes in v5:
time: 82.5 us; the launch traced here: 82.3 us
  Pallas kernels  81.7 us (99%)
    pallas_call x1, Pallas kernels, on_device(): pl.pallas_call(kernel, out_shape=(pltpu.VMEM(peers, F32), pltpu.VMEM((GRO...  79.8 us
    pallas_call x1, Pallas kernels, on_device(): pl.pallas_call(finish, out_shape=(jax.ShapeDtypeStruct((ROWS, WIDTH), F32...  1.93 us

profile of v5, /device:TPU:0, one launch (start us, length us, event | category | flops | bytes accessed | tf_op | source)
XLA Modules:
  0.0 82.3 jit_solution(15289987275681363466)
XLA Ops:
  0.6 79.8 %shard_map.93 = (f32[64,32,256]{2,1,0:T(8,128)S(1)}, bf16[4,1024,512]{2,1,0:T(8,128)(2,1)S(1)}, f32[1024,256]{1,0:T(8,128)S(1)}, f32[7,128,256]{2,1,0:T(8,128)S(...) custom-call(s32[1,1024]{1,0:T(1,128)} %bitcast.19, f32[1024,256]{1,0:T(8,128)} %samples.1, ...), custom_call_target="tpu_custom_call" | custom-call | flops 16106127360 | bytes 8388608 | tf_op jit(solution)/shard_map/pallas_call | solution.py:318
  80.4 1.9 %shard_map.94 = (f32[1024,256]{1,0:T(8,128)}, f32[7,128,256]{2,1,0:T(8,128)}, f32[7,128,256]{2,1,0:T(8,128)}, f32[7,128,256]{2,1,0:T(8,128)}) custom-call(f32[64,32,256]{2,1,0:T(8,128)S(1)} %get-tuple-element.14.ret, bf16[4,1024,512]{2,1,0:T(8,128)(2,1)S(1)} %get-tuple-element.15.place, f32[1024,256]{1,0:T(8,128)S(1)} %get-tuple-element.16.partial, ...), custom_call_target="tpu_custom_call" | custom-call | tf_op jit(solution)/shard_map/pallas_call | solution.py:368
